TPU v7x, 32 devices: a whole 2x2x4 slice. The times are simulated.
32 devices in a mesh: group: 2 (over x), row: 16 (over z, y, core).
Axes of the slice: x: 2, y: 2, z: 4, core: 2. Of those that a mesh axis runs over, the one named last changes fastest.
Arguments:
- sources: float32 [4, 16, 8192], P('group', None, 'row'), parts along dimension 0, may hold values from -6 to 6
- lower_sources: float32 [4, 16, 8192], P('group', None, 'row'), parts along dimension 0, may hold values from -6 to 6
- upper_operator: float32 [16384, 8192], P(('group', 'row')), parts along dimension 0, may hold values from -0.0625 to 0.0625
- lower_operator: float32 [16384, 8192], P(('group', 'row')), parts along dimension 0, may hold values from -0.0625 to 0.0625
- upper_impedance: float32 [16384], P(('group', 'row')), parts along dimension 0, may hold values from 0.5 to 2
- lower_impedance: float32 [16384], P(('group', 'row')), parts along dimension 0, may hold values from 0.5 to 2
Outputs:
- lower_field: float32 [4, 16, 8192], P('group', None, 'row'), parts along dimension 0
- reflected: float32 [4, 16, 8192], P('group', None, 'row'), parts along dimension 0
There are 2 independent parts, one for each index of `group`. A program takes and returns all parts, laid end to end along the dimension named above; each array names one. Nothing has to cross between parts.
All inputs are finite; a program needn't handle non-finite values.
Results may differ from a plain program's by a relative error of at most 0.000098.
Values sent between devices are 32-bit elements; how exact they have to be, the bound alone decides.
A program may use at most 64 MiB of HBM per device.

v0:
```python
import jax
from jax import lax
from jax.sharding import PartitionSpec as P


def apply_rows(piece, operator):
    return lax.dot_general(
        piece, operator, (((1,), (1,)), ((), ())), precision=lax.Precision.HIGHEST
    )


def transposed_term(operator, traces):
    return lax.dot_general(
        operator, traces, (((0,), (1,)), ((), ())), precision=lax.Precision.HIGHEST
    )


def body(sources, lower_sources, upper_operator, lower_operator, upper_impedance, lower_impedance):
    batch_count, column_count, local_rows = sources.shape
    entering = sources.reshape(batch_count * column_count, local_rows)
    inside = lower_sources.reshape(batch_count * column_count, local_rows)
    downward = apply_rows(
        lax.all_gather(entering, "row", axis=1, tiled=True), operator=upper_operator
    )
    lower_field = apply_rows(
        lax.all_gather(downward, "row", axis=1, tiled=True), operator=lower_operator
    )
    scaled = lower_impedance * lower_field + inside
    bounced = lax.psum_scatter(
        transposed_term(lower_operator, scaled), "row", scatter_dimension=0, tiled=True
    ).T
    mixed = upper_impedance * bounced - downward
    reflected = lax.psum_scatter(
        transposed_term(upper_operator, mixed), "row", scatter_dimension=0, tiled=True
    ).T
    return (
        lower_field.reshape(batch_count, column_count, local_rows),
        reflected.reshape(batch_count, column_count, local_rows),
    )


def solution(mesh):
    placed = (
        P("group", None, "row"),
        P("group", None, "row"),
        P(("group", "row"), None),
        P(("group", "row"), None),
        P(("group", "row")),
        P(("group", "row")),
    )
    return jax.shard_map(
        body,
        mesh=mesh,
        in_specs=placed,
        out_specs=(P("group", None, "row"), P("group", None, "row")),
        check_vma=False,
    )
```

profile of v0, /device:TPU:0, one launch (start us, length us, event | category | flops | bytes accessed | tf_op | source)
XLA Modules:
  0.0 273.4 jit_solution(13786592155926288520)
XLA Ops:
  7.2 0.0 copy-start.2
  7.2 0.0 copy-start.1
  7.2 0.0 all-gather.3.cloned.1.call-start
  7.2 0.7 all-gather.3.cloned.1.call-update
  7.9 0.0 all-gather.5.cloned.1.call-start
  8.0 42.9 %all-gather.3.cloned.1.call-done = f32[32,8192]{1,0:T(8,128)} async-done(((f32[32,512]{1,0:T(8,128)}), f32[32,8192]{1,0:T(8,128)}) %all-gather.3.cloned.1.call-update) | async-done | bytes 1048592 | tf_op jit(solution)/shard_map/all_gather | solution.py:23
  50.9 18.9 %fusion.2 = f32[32,512]{1,0:T(8,128)} fusion(f32[32,8192]{1,0:T(8,128)} %all-gather.3.cloned.1.call-done, f32[512,8192]{1,0:T(8,128)} %param.8), kind=kOutput, calls=%fused_computation.6 | convolution fusion | flops 1610612736 | bytes 17891328 | tf_op jit(solution)/shard_map/dot_general | solution.py:7
  69.8 0.0 all-gather.5.cloned.1.call-update
  69.9 0.0 copy-start
  69.9 0.0 copy-start.3
  69.9 0.2 reduce-scatter.3.cloned.1.call-start
  70.1 36.8 %all-gather.5.cloned.1.call-done = f32[32,8192]{1,0:T(8,128)} async-done(((f32[32,512]{1,0:T(8,128)}), f32[32,8192]{1,0:T(8,128)}) %all-gather.5.cloned.1.call-update) | async-done | bytes 1048592 | tf_op jit(solution)/shard_map/all_gather | solution.py:26
  106.9 0.0 copy-done.2
  106.9 0.0 copy-done.1
  106.9 19.0 %bitcast_add_fusion = (f32[32,512]{1,0:T(8,128)S(1)}, f32[32,512]{1,0:T(8,128)}) fusion(f32[2,16,512]{2,1,0:T(8,128)S(1)} %copy-done.1, f32[512]{0:T(512)S(1)} %copy-done.2, f32[32,8192]{1,0:T(8,128)} %all-gather.5.cloned.1.call-done, f32[512,8192]{1,0:T(8,128)} %param.9), kind=kOutput, calls=%fused_computation.3 | convolution fusion | flops 1610645504 | bytes 18024448 | tf_op jit(solution)/shard_map/dot_general | solution.py:7
  125.9 14.1 %convolution_bitcast_fusion.1 = f32[8192,32]{0,1:T(8,128)} fusion(f32[32,512]{1,0:T(8,128)S(1)} %get-tuple-element.2, f32[512,8192]{1,0:T(8,128)} %param.9), kind=kOutput, calls=%fused_computation.1 | convolution fusion | flops 1610612736 | bytes 17891328 | tf_op jit(solution)/shard_map/dot_general | solution.py:13
  140.0 0.0 reduce-scatter.3.cloned.1.call-update
  140.0 0.3 reduce-scatter.5.cloned.1.call-start
  140.2 56.2 %reduce-scatter.3.cloned.1.call-done = f32[512,32]{0,1:T(8,128)} async-done(((f32[8192,32]{0,1:T(8,128)}), f32[512,32]{0,1:T(8,128)}) %reduce-scatter.3.cloned.1.call-update) | async-done | bytes 65552 | tf_op jit(solution)/shard_map/reduce_scatter | solution.py:29
  196.5 0.0 copy-done
  196.5 0.0 copy-done.3
  196.5 13.9 %convolution_bitcast_fusion = f32[8192,32]{0,1:T(8,128)} fusion(f32[512,8192]{1,0:T(8,128)} %param.8, f32[32,512]{1,0:T(8,128)S(1)} %copy-done, f32[512,32]{0,1:T(8,128)} %reduce-scatter.3.cloned.1.call-done, f32[512]{0:T(512)S(1)} %copy-done.3), kind=kOutput, calls=%fused_computation | convolution fusion | flops 1610645504 | bytes 17958912 | tf_op jit(solution)/shard_map/dot_general | solution.py:13
  210.3 0.0 reduce-scatter.5.cloned.1.call-update
  210.4 56.5 %reduce-scatter.5.cloned.1.call-done = f32[512,32]{0,1:T(8,128)} async-done(((f32[8192,32]{0,1:T(8,128)}), f32[512,32]{0,1:T(8,128)}) %reduce-scatter.5.cloned.1.call-update) | async-done | bytes 65552 | tf_op jit(solution)/shard_map/reduce_scatter | solution.py:33
Async XLA Ops:
  7.2 99.7 %copy-start.2 = (f32[512]{0:T(512)S(1)}, f32[512]{0:T(512)}, u32[]{:S(2)}) copy-start(f32[512]{0:T(512)} %param.11) | copy-start | bytes 6148
  7.2 99.7 %copy-start.1 = (f32[2,16,512]{2,1,0:T(8,128)S(1)}, f32[2,16,512]{2,1,0:T(8,128)}, u32[]{:S(2)}) copy-start(f32[2,16,512]{2,1,0:T(8,128)} %param.7) | copy-start | bytes 196612
  7.2 43.7 %all-gather.3.cloned.1.call-start = ((), (), s32[]{:S(2)}) async-start(), calls=%async_computation.2 | async-start | bytes 1114112 | tf_op jit(solution)/shard_map/all_gather | solution.py:23
  7.9 99.0 %all-gather.5.cloned.1.call-start = ((), (), s32[]{:S(2)}) async-start(), calls=%async_computation.3 | async-start | bytes 1114112 | tf_op jit(solution)/shard_map/all_gather | solution.py:26
  69.9 126.6 %copy-start = (f32[32,512]{1,0:T(8,128)S(1)}, f32[32,512]{1,0:T(8,128)}, u32[]{:S(2)}) copy-start(f32[32,512]{1,0:T(8,128)} %fusion.2) | copy-start | bytes 196612
  69.9 126.6 %copy-start.3 = (f32[512]{0:T(512)S(1)}, f32[512]{0:T(512)}, u32[]{:S(2)}) copy-start(f32[512]{0:T(512)} %param.10) | copy-start | bytes 6148
  69.9 126.6 %reduce-scatter.3.cloned.1.call-start = ((), (), s32[]{:S(2)}) async-start(), calls=%async_computation.4 | async-start | bytes 1114112 | tf_op jit(solution)/shard_map/reduce_scatter | solution.py:29
  140.0 126.9 %reduce-scatter.5.cloned.1.call-start = ((), (), s32[]{:S(2)}) async-start(), calls=%async_computation.5 | async-start | bytes 1114112 | tf_op jit(solution)/shard_map/reduce_scatter | solution.py:33
Sparse Core Ops, SparseCore 0:
  10.2 40.6 all-gather.2
  70.0 36.8 all-gather.4
  140.1 56.3 reduce-scatter.2
  210.5 56.3 reduce-scatter.4
where the time goes:
time: 274 us; the launch traced here: 273 us
  waiting for transfers between devices  193 us (70%)
  matrix products  65.9 us (24%)
  between operations  13.8 us (5%)
    reduce_scatter x1, waiting for transfers between devices, body(): lax.psum_scatter(transposed_term(upper_operator, mixed), 'row', scatter_d...  56.5 us
    reduce_scatter x1, waiting for transfers between devices, body(): lax.psum_scatter(transposed_term(lower_operator, scaled), 'row', scatter_...  56.2 us
    all_gather x1, waiting for transfers between devices, body(): lax.all_gather(entering, 'row', axis=1, tiled=True)  42.9 us
    dot_general x2, matrix products, apply_rows(): lax.dot_general(piece, operator, (((1,), (1,)), ((), ())), precision=lax....  37.9 us
    all_gather x1, waiting for transfers between devices, body(): lax.all_gather(downward, 'row', axis=1, tiled=True)  36.8 us
    dot_general x2, matrix products, transposed_term(): lax.dot_general(operator, traces, (((0,), (1,)), ((), ())), precision=lax...  27.9 us
  transfers between devices with their start and end apart: 4, of which 4 were waited for; matrix products, arithmetic and copies ran while one was open for 0% of the time, Pallas kernels for 0%

commit v1 on v0

v1 whole, which is shorter than its diff:
```python
import functools

import jax
import jax.numpy as jnp
from jax import lax
from jax.experimental import pallas as pl
from jax.experimental.pallas import tpu as pltpu
from jax.sharding import PartitionSpec as P

MESH = pl.DeviceIdType.MESH
F32, BF16 = jnp.float32, jnp.bfloat16
NT = (((1,), (1,)), ((), ()))
NN = (((1,), (0,)), ((), ()))


def split(value):
    high = value.astype(BF16)
    return high, (value - high.astype(F32)).astype(BF16)


def stacked(value):
    high, low = split(value)
    return jnp.concatenate([high, low], axis=0), high


def product(both, high, operator_high, operator_low, dims):
    rows = high.shape[0]
    main = lax.dot_general(both, operator_high, dims, preferred_element_type=F32)
    rest = lax.dot_general(high, operator_low, dims, preferred_element_type=F32)
    return main[:rows] + main[rows:] + rest


def kernel(lines, sides, cores, source_ref, inside_ref, upper_hbm, lower_hbm, upper_gain, lower_gain,
           field_ref, reflected_ref,
           stage, upper_high, upper_low, lower_high, lower_low, gathered, down_ref,
           core_out, core_in, side_out, side_in, line_out, line_in,
           load_sem, gather_send, gather_recv, core_send, core_recv, side_send, side_recv, line_send, line_recv):
    size = source_ref.shape[1]
    me = lax.axis_index("row")
    core = lax.rem(me, cores)
    side = lax.rem(me // cores, sides)
    line = me // (cores * sides)

    def at(dz, dy, dc):
        return (lax.rem(line + dz, lines) * sides + lax.rem(side + dy, sides)) * cores + lax.rem(core + dc, cores)

    def slot_of(dz, dy, dc):
        return (dz * sides + dy) * cores + dc

    slots = [(dz, dy, dc) for dz in range(lines) for dy in range(sides) for dc in range(cores)]

    def load(operator, which, key):
        slot = slot_of(*key)
        columns = pl.ds(pl.multiple_of(at(*key) * size, size), size)
        copy = pltpu.make_async_copy(operator.at[:, columns], stage.at[slot], load_sem.at[which, slot])
        copy.start()
        return copy

    upper_loads = [load(upper_hbm, 0, key) for key in slots]

    partners = [at(0, 0, 1), at(0, 1, 0)] + [at(dz, 0, 0) for dz in range(1, lines)]
    barrier = pltpu.get_barrier_semaphore()
    for partner in partners:
        pl.semaphore_signal(barrier, inc=1, device_id={"row": partner}, device_id_type=MESH)
    pl.semaphore_wait(barrier, len(partners))

    started = []

    def send(src, dst, send_sem, recv_sem, target):
        copy = pltpu.make_async_remote_copy(
            src_ref=src, dst_ref=dst, send_sem=send_sem, recv_sem=recv_sem,
            device_id={"row": target}, device_id_type=MESH)
        copy.start()
        started.append(copy)
        return copy

    def divide(slot, high_ref, low_ref):
        chunk = min(64, size)

        def part(step, carry):
            rows = pl.ds(pl.multiple_of(step * chunk, chunk), chunk)
            high, low = split(stage[slot, rows, :])
            high_ref[slot, rows, :] = high
            low_ref[slot, rows, :] = low
            return carry

        lax.fori_loop(0, size // chunk, part, 0)

    def gather_apply(phase, own, high_ref, low_ref, loads, after):
        copies = {}

        def give(src, key, target):
            slot = slot_of(*key)
            copies[key] = send(src, gathered.at[phase, slot], gather_send.at[phase, slot],
                               gather_recv.at[phase, slot], target)

        give(own, (0, 0, 1), at(0, 0, 1))
        give(own, (0, 1, 0), at(0, 1, 0))
        for dz in range(1, lines):
            give(own, (dz, 0, 0), at(lines - dz, 0, 0))
        total = None
        for key in slots:
            dz, dy, dc = key
            slot = slot_of(*key)
            block = own
            if slot:
                copies[key].wait_recv()
                block = gathered.at[phase, slot]
                if dc == 0:
                    if dy == 0:
                        give(block, (dz, 1, 0), at(0, 1, 0))
                    give(block, (dz, dy, 1), at(0, 0, 1))
            loads[slot].wait()
            divide(slot, high_ref, low_ref)
            after(key)
            both, high = stacked(block[...])
            term = product(both, high, high_ref[slot], low_ref[slot], NT)
            total = term if total is None else total + term
        return total

    def scatter_apply(phase, value, high_ref, low_ref):
        both, high = stacked(value)

        def part(dz, dy, dc):
            slot = slot_of(dz, dy, dc)
            return product(both, high, high_ref[slot], low_ref[slot], NN)

        def to_core(dz, dy):
            slot = dz * sides + dy
            core_out[phase, slot] = part(dz, dy, 1)
            return send(core_out.at[phase, slot], core_in.at[phase, slot], core_send.at[phase, slot],
                        core_recv.at[phase, slot], at(0, 0, 1))

        side_copies, line_copies = {}, {}

        def finish(dz):
            side_copies[dz].wait_recv()
            line_out[phase, dz] = line_out[phase, dz] + side_in[phase, dz]
            line_copies[dz] = send(line_out.at[phase, dz], line_in.at[phase, dz], line_send.at[phase, dz],
                                   line_recv.at[phase, dz], at(dz, 0, 0))

        pending = None
        for dz in list(range(1, lines)) + [0]:
            other = to_core(dz, 1)
            same = to_core(dz, 0)
            mine = part(dz, 1, 0)
            other.wait_recv()
            side_out[phase, dz] = mine + core_in[phase, dz * sides + 1]
            side_copies[dz] = send(side_out.at[phase, dz], side_in.at[phase, dz], side_send.at[phase, dz],
                                   side_recv.at[phase, dz], at(0, 1, 0))
            mine = part(dz, 0, 0)
            if pending is not None:
                finish(pending)
            same.wait_recv()
            line_out[phase, dz] = mine + core_in[phase, dz * sides]
            pending = dz
        side_copies[0].wait_recv()
        total = line_out[phase, 0] + side_in[phase, 0]
        for dz in range(1, lines):
            line_copies[dz].wait_recv()
            total = total + line_in[phase, dz]
        return total

    lower_loads = {}

    def load_lower(key):
        lower_loads[slot_of(*key)] = load(lower_hbm, 1, key)

    down_ref[...] = gather_apply(0, source_ref, upper_high, upper_low, upper_loads, load_lower)
    field = gather_apply(1, down_ref, lower_high, lower_low, lower_loads, lambda key: None)
    field_ref[...] = field
    scaled = lower_gain[...] * field + inside_ref[...]
    bounced = scatter_apply(0, scaled, lower_high, lower_low)
    mixed = upper_gain[...] * bounced - down_ref[...]
    reflected_ref[...] = scatter_apply(1, mixed, upper_high, upper_low)
    for copy in started:
        copy.wait_send()


def body(devices, sources, lower_sources, upper_operator, lower_operator, upper_impedance, lower_impedance):
    batch_count, column_count, size = sources.shape
    columns = batch_count * column_count
    cores, sides = 2, 2
    lines = devices // (cores * sides)
    vmem, dma = pltpu.VMEM, pltpu.SemaphoreType.DMA
    traces = jax.ShapeDtypeStruct((columns, size), F32)
    whole = pl.BlockSpec(memory_space=pltpu.VMEM)
    remote = pl.BlockSpec(memory_space=pl.ANY)
    field, reflected = pl.pallas_call(
        functools.partial(kernel, lines, sides, cores),
        out_shape=(traces, traces),
        in_specs=[whole, whole, remote, remote, whole, whole],
        out_specs=(whole, whole),
        scratch_shapes=[
            vmem((devices, size, size), F32),
            vmem((devices, size, size), BF16),
            vmem((devices, size, size), BF16),
            vmem((devices, size, size), BF16),
            vmem((devices, size, size), BF16),
            vmem((2, devices, columns, size), F32),
            vmem((columns, size), F32),
            vmem((2, lines * sides, columns, size), F32),
            vmem((2, lines * sides, columns, size), F32),
            vmem((2, lines, columns, size), F32),
            vmem((2, lines, columns, size), F32),
            vmem((2, lines, columns, size), F32),
            vmem((2, lines, columns, size), F32),
            dma((2, devices)),
            dma((2, devices)),
            dma((2, devices)),
            dma((2, lines * sides)),
            dma((2, lines * sides)),
            dma((2, lines)),
            dma((2, lines)),
            dma((2, lines)),
            dma((2, lines)),
        ],
        compiler_params=pltpu.CompilerParams(
            collective_id=0, has_side_effects=True, vmem_limit_bytes=60 * 1024 * 1024),
    )(
        sources.reshape(columns, size),
        lower_sources.reshape(columns, size),
        upper_operator,
        lower_operator,
        upper_impedance.reshape(1, size),
        lower_impedance.reshape(1, size),
    )
    shape = (batch_count, column_count, size)
    return field.reshape(shape), reflected.reshape(shape)


def solution(mesh):
    placed = (
        P("group", None, "row"),
        P("group", None, "row"),
        P(("group", "row"), None),
        P(("group", "row"), None),
        P(("group", "row")),
        P(("group", "row")),
    )
    return jax.shard_map(
        functools.partial(body, mesh.shape["row"]),
        mesh=mesh,
        in_specs=placed,
        out_specs=(P("group", None, "row"), P("group", None, "row")),
        check_vma=False,
    )
```

time: 274 us -> 77.7 us (0.28)
  waiting for transfers between devices: 193 us -> 0 us
  Pallas kernels: 0 us -> 73.8 us
  matrix products: 65.9 us -> 0 us
  between operations: 13.8 us -> 0.64 us
  local copies, waits for them, and re-layouts: 0.02 us -> 2.95 us
    reduce_scatter x2 -> x0, waiting for transfers between devices: 113 us -> none  [the longest x1 56.5 us: body(): lax.psum_scatter(transposed_term(upper_operator, mixed), 'row', scatter_d...]
    all_gather x2 -> x0, waiting for transfers between devices: 79.7 us -> none  [the longest x1 42.9 us: body(): lax.all_gather(entering, 'row', axis=1, tiled=True)]
    pallas_call x0 -> x1, Pallas kernels: none -> 73.8 us  [body(): pl.pallas_call(functools.partial(kernel, lines, sides, cores), out_shape=...]
    dot_general x4 -> x0, matrix products: 65.9 us -> none  [the longest x2 37.9 us: apply_rows(): lax.dot_general(piece, operator, (((1,), (1,)), ((), ())), precision=lax....]
    unnamed x8 -> x2, local copies, waits for them, and re-layouts: 0.02 us -> 2.95 us
  transfers between devices with their start and end apart: 4 -> 0, of which waited for: 4 -> 0; matrix products, arithmetic and copies ran while one was open for 0% -> 0% of each run, Pallas kernels for 0% -> 0%
where the time goes in v1:
time: 77.7 us; the launch traced here: 77.4 us
  Pallas kernels  73.8 us (95%)
  local copies, waits for them, and re-layouts  2.95 us (4%)
    pallas_call x1, Pallas kernels, body(): pl.pallas_call(functools.partial(kernel, lines, sides, cores), out_shape=...  73.8 us
    unnamed x2, local copies, waits for them, and re-layouts  2.95 us

profile of v1, /device:TPU:0, one launch (start us, length us, event | category | flops | bytes accessed | tf_op | source)
XLA Modules:
  0.0 77.4 jit_solution(13424389791541301606)
XLA Ops:
  0.6 73.8 %shard_map.77 = (f32[32,512]{1,0:T(8,128)}, f32[32,512]{1,0:T(8,128)}) custom-call(f32[32,512]{1,0:T(8,128)} %bitcast.6, f32[32,512]{1,0:T(8,128)} %bitcast.7, f32[512,8192]{1,0:T(8,128)} %upper_hbm.1, f32[512,8192]{1,0:T(8,128)} %lower_hbm.1, f32[1,512]{1,0:T(1,128)} %bitcast.10, f32[1,512]{1,0:T(1,128)} %bitcast.11), custom_call_target="tpu_custom_call" | custom-call | tf_op jit(solution)/shard_map/pallas_call | solution.py:189
  74.5 1.5 %copy.10 = f32[2,16,512]{2,1,0:T(8,128)} copy(f32[2,16,512]{2,1,0:T(8,128)} %bitcast.9) | data formatting | bytes 131072
  76.0 1.5 %copy.11 = f32[2,16,512]{2,1,0:T(8,128)} copy(f32[2,16,512]{2,1,0:T(8,128)} %bitcast.8) | data formatting | bytes 131072

commit v2 on v1

v2 whole, which is shorter than its diff:
```python
import functools

import jax
import jax.numpy as jnp
from jax import lax
from jax.experimental import pallas as pl
from jax.experimental.pallas import tpu as pltpu
from jax.sharding import PartitionSpec as P

MESH = pl.DeviceIdType.MESH
F32, BF16 = jnp.float32, jnp.bfloat16
NT = (((1,), (1,)), ((), ()))
NN = (((1,), (0,)), ((), ()))


def split(value):
    high = value.astype(BF16)
    return high, (value - high.astype(F32)).astype(BF16)


def stacked(value):
    high, low = split(value)
    return jnp.concatenate([high, low], axis=0), high


def folded(value):
    rows = value.shape[0] // 2
    return value[:rows] + value[rows:]


def kernel(lines, sides, cores, source_ref, inside_ref, upper_hbm, lower_hbm, upper_gain, lower_gain,
           field_ref, reflected_ref,
           stage, upper, lower, gathered, down_ref, sums,
           core_out, core_in, side_out, side_in, line_out, line_in,
           load_sem, gather_send, gather_recv, core_send, core_recv, side_send, side_recv, line_send, line_recv):
    size = source_ref.shape[1]
    me = lax.axis_index("row")
    core = lax.rem(me, cores)
    side = lax.rem(me // cores, sides)
    line = me // (cores * sides)

    def at(dz, dy, dc):
        return (lax.rem(line + dz, lines) * sides + lax.rem(side + dy, sides)) * cores + lax.rem(core + dc, cores)

    def slot_of(dz, dy, dc):
        return (dz * sides + dy) * cores + dc

    slots = [(dz, dy, dc) for dz in range(lines) for dy in range(sides) for dc in range(cores)]

    def load(operator, which, key):
        slot = slot_of(*key)
        columns = pl.ds(pl.multiple_of(at(*key) * size, size), size)
        copy = pltpu.make_async_copy(operator.at[:, columns], stage.at[slot], load_sem.at[which, slot])
        copy.start()
        return copy

    upper_loads = [load(upper_hbm, 0, key) for key in slots]

    partners = [at(0, 0, 1), at(0, 1, 0)] + [at(dz, 0, 0) for dz in range(1, lines)]
    barrier = pltpu.get_barrier_semaphore()
    for partner in partners:
        pl.semaphore_signal(barrier, inc=1, device_id={"row": partner}, device_id_type=MESH)
    pl.semaphore_wait(barrier, len(partners))

    started = []

    def send(src, dst, send_sem, recv_sem, target):
        copy = pltpu.make_async_remote_copy(
            src_ref=src, dst_ref=dst, send_sem=send_sem, recv_sem=recv_sem,
            device_id={"row": target}, device_id_type=MESH)
        copy.start()
        started.append(copy)
        return copy

    def gather_apply(phase, own, parts, loads, after):
        copies = {}
        chunk = min(256, size)

        def give(src, key, target):
            slot = slot_of(*key)
            copies[key] = send(src, gathered.at[phase, slot], gather_send.at[phase, slot],
                               gather_recv.at[phase, slot], target)

        def arrive(key):
            dz, dy, dc = key
            slot = slot_of(*key)
            copies[key].wait_recv()
            if dc == 0:
                if dy == 0:
                    give(gathered.at[phase, slot], (dz, 1, 0), at(0, 1, 0))
                give(gathered.at[phase, slot], (dz, dy, 1), at(0, 0, 1))

        def add(keys):
            for key in keys:
                loads[slot_of(*key)].wait()
            for key in keys:
                slot = slot_of(*key)
                both = stacked(gathered[phase, slot] if slot else own[...])[0]
                for begin in range(0, size, chunk):
                    high, low = split(stage[slot, begin:begin + chunk, :])
                    parts[slot, begin:begin + chunk, :] = high
                    parts[slot, size + begin:size + begin + chunk, :] = low
                    term = folded(lax.dot_general(
                        jnp.concatenate([high, low], axis=0), both, NT, preferred_element_type=F32))
                    if slot:
                        sums[begin:begin + chunk, :] += term
                    else:
                        sums[begin:begin + chunk, :] = term
            for key in keys:
                after(key)

        for dz in range(1, lines):
            give(own, (dz, 0, 0), at(lines - dz, 0, 0))
        give(own, (0, 1, 0), at(0, 1, 0))
        give(own, (0, 0, 1), at(0, 0, 1))
        add([(0, 0, 0)])
        late = (0, 0, 1)
        for dz in range(lines):
            for dy in range(sides):
                if dz or dy:
                    arrive((dz, dy, 0))
                    arrive(late)
                    add([(dz, dy, 0), late])
                    late = (dz, dy, 1)
        arrive(late)
        add([late])
        return folded(sums[...].T)

    def scatter_apply(phase, value, parts):
        both = stacked(value)[0]
        both = jnp.concatenate([both, both], axis=1)

        def part(dz, dy, dc):
            return folded(lax.dot_general(both, parts[slot_of(dz, dy, dc)], NN, preferred_element_type=F32))

        core_copies, side_copies, line_copies = {}, {}, {}

        def compute(dz, dy):
            slot = dz * sides + dy
            other = part(dz, dy, 1)
            mine = part(dz, dy, 0)
            core_out[phase, slot] = other
            core_copies[dz, dy] = send(
                core_out.at[phase, slot], core_in.at[phase, slot], core_send.at[phase, slot],
                core_recv.at[phase, slot], at(0, 0, 1))
            (side_out if dy else line_out)[phase, dz] = mine

        def merge(dz, dy):
            out = side_out if dy else line_out
            core_copies[dz, dy].wait_recv()
            out[phase, dz] = out[phase, dz] + core_in[phase, dz * sides + dy]
            if dy:
                side_copies[dz] = send(side_out.at[phase, dz], side_in.at[phase, dz], side_send.at[phase, dz],
                                       side_recv.at[phase, dz], at(0, 1, 0))

        def finish(dz):
            side_copies[dz].wait_recv()
            line_out[phase, dz] = line_out[phase, dz] + side_in[phase, dz]
            if dz:
                line_copies[dz] = send(line_out.at[phase, dz], line_in.at[phase, dz], line_send.at[phase, dz],
                                       line_recv.at[phase, dz], at(dz, 0, 0))

        far = list(range(1, lines)) + [0]
        order = [(far[0], 1)]
        for before, now in zip(far, far[1:]):
            order += [(now, 1), (before, 0)]
        order += [(0, 0)]
        merged = []
        for step, key in enumerate(order):
            compute(*key)
            if merged:
                finish(merged.pop())
            if step:
                merge(*order[step - 1])
                if order[step - 1][1] == 0:
                    merged.append(order[step - 1][0])
        for dz in merged:
            finish(dz)
        merge(*order[-1])
        finish(0)
        total = line_out[phase, 0]
        for dz in range(1, lines):
            line_copies[dz].wait_recv()
            total = total + line_in[phase, dz]
        return total

    lower_loads = {}

    def load_lower(key):
        lower_loads[slot_of(*key)] = load(lower_hbm, 1, key)

    down_ref[...] = gather_apply(0, source_ref, upper, upper_loads, load_lower)
    field = gather_apply(1, down_ref, lower, lower_loads, lambda key: None)
    field_ref[...] = field
    scaled = lower_gain[...] * field + inside_ref[...]
    bounced = scatter_apply(0, scaled, lower)
    mixed = upper_gain[...] * bounced - down_ref[...]
    reflected_ref[...] = scatter_apply(1, mixed, upper)
    for copy in started:
        copy.wait_send()


def write(field_in, reflected_in, field_out, reflected_out, sems):
    first = pltpu.make_async_copy(field_in, field_out, sems.at[0])
    second = pltpu.make_async_copy(reflected_in, reflected_out, sems.at[1])
    first.start()
    second.start()
    first.wait()
    second.wait()


def body(devices, sources, lower_sources, upper_operator, lower_operator, upper_impedance, lower_impedance):
    batch_count, column_count, size = sources.shape
    columns = batch_count * column_count
    cores, sides = 2, 2
    lines = devices // (cores * sides)
    vmem, dma = pltpu.VMEM, pltpu.SemaphoreType.DMA
    traces = jax.ShapeDtypeStruct((columns, size), F32)
    whole = pl.BlockSpec(memory_space=pltpu.VMEM)
    remote = pl.BlockSpec(memory_space=pl.ANY)
    field, reflected = pl.pallas_call(
        functools.partial(kernel, lines, sides, cores),
        out_shape=(traces, traces),
        in_specs=[whole, whole, remote, remote, whole, whole],
        out_specs=(whole, whole),
        scratch_shapes=[
            vmem((devices, size, size), F32),
            vmem((devices, 2 * size, size), BF16),
            vmem((devices, 2 * size, size), BF16),
            vmem((2, devices, columns, size), F32),
            vmem((columns, size), F32),
            vmem((size, 2 * columns), F32),
            vmem((2, lines * sides, columns, size), F32),
            vmem((2, lines * sides, columns, size), F32),
            vmem((2, lines, columns, size), F32),
            vmem((2, lines, columns, size), F32),
            vmem((2, lines, columns, size), F32),
            vmem((2, lines, columns, size), F32),
            dma((2, devices)),
            dma((2, devices)),
            dma((2, devices)),
            dma((2, lines * sides)),
            dma((2, lines * sides)),
            dma((2, lines)),
            dma((2, lines)),
            dma((2, lines)),
            dma((2, lines)),
        ],
        compiler_params=pltpu.CompilerParams(
            collective_id=0, has_side_effects=True, vmem_limit_bytes=60 * 1024 * 1024),
    )(
        sources.reshape(columns, size),
        lower_sources.reshape(columns, size),
        upper_operator,
        lower_operator,
        upper_impedance.reshape(1, size),
        lower_impedance.reshape(1, size),
    )
    field, reflected = pl.pallas_call(
        write,
        out_shape=(traces, traces),
        in_specs=[remote, remote],
        out_specs=(remote, remote),
        scratch_shapes=[dma((2,))],
    )(field, reflected)
    shape = (batch_count, column_count, size)
    return field.reshape(shape), reflected.reshape(shape)


def solution(mesh):
    placed = (
        P("group", None, "row"),
        P("group", None, "row"),
        P(("group", "row"), None),
        P(("group", "row"), None),
        P(("group", "row")),
        P(("group", "row")),
    )
    return jax.shard_map(
        functools.partial(body, mesh.shape["row"]),
        mesh=mesh,
        in_specs=placed,
        out_specs=(P("group", None, "row"), P("group", None, "row")),
        check_vma=False,
    )
```

time: 77.7 us -> 74.1 us (0.954)
  local copies, waits for them, and re-layouts: 2.95 us -> 0 us
    pallas_call x1, Pallas kernels: 73.8 us -> 68 us  [body(): pl.pallas_call(functools.partial(kernel, lines, sides, cores), out_shape=...]
    pallas_call x0 -> x1, Pallas kernels: none -> 5.09 us  [body(): pl.pallas_call(write, out_shape=(traces, traces), in_specs=[remote, remot...]
    unnamed x2 -> x0, local copies, waits for them, and re-layouts: 2.95 us -> none
where the time goes in v2:
time: 74.1 us; the launch traced here: 73.9 us
  Pallas kernels  73.1 us (99%)
  between operations  0.8 us (1%)
    pallas_call x1, Pallas kernels, body(): pl.pallas_call(functools.partial(kernel, lines, sides, cores), out_shape=...  68 us
    pallas_call x1, Pallas kernels, body(): pl.pallas_call(write, out_shape=(traces, traces), in_specs=[remote, remot...  5.09 us

profile of v2, /device:TPU:0, one launch (start us, length us, event | category | flops | bytes accessed | tf_op | source)
XLA Modules:
  0.0 73.9 jit_solution(3267344696084404740)
XLA Ops:
  0.6 68.0 %shard_map.77 = (f32[32,512]{1,0:T(8,128)}, f32[32,512]{1,0:T(8,128)}) custom-call(f32[32,512]{1,0:T(8,128)} %bitcast.6, f32[32,512]{1,0:T(8,128)} %bitcast.7, f32[512,8192]{1,0:T(8,128)} %upper_hbm.1, f32[512,8192]{1,0:T(8,128)} %lower_hbm.1, f32[1,512]{1,0:T(1,128)} %bitcast.8, f32[1,512]{1,0:T(1,128)} %bitcast.9), custom_call_target="tpu_custom_call" | custom-call | tf_op jit(solution)/shard_map/pallas_call | solution.py:221
  68.7 5.1 %shard_map.78 = (f32[32,512]{1,0:T(8,128)}, f32[32,512]{1,0:T(8,128)}) custom-call(f32[32,512]{1,0:T(8,128)} %get-tuple-element.6.field_in, f32[32,512]{1,0:T(8,128)} %get-tuple-element.7.reflected_in), custom_call_target="tpu_custom_call" | custom-call | tf_op jit(solution)/shard_map/pallas_call | solution.py:259

commit v3 on v0

v3 whole, which is shorter than its diff:
```python
import functools

import jax
import jax.numpy as jnp
from jax import lax
from jax.experimental import pallas as pl
from jax.experimental.pallas import tpu as pltpu
from jax.sharding import PartitionSpec as P

MESH = pl.DeviceIdType.MESH
F32, BF16 = jnp.float32, jnp.bfloat16
NT = (((1,), (1,)), ((), ()))
NN = (((1,), (0,)), ((), ()))


def split(value):
    high = value.astype(BF16)
    return high, (value - high.astype(F32)).astype(BF16)


def stacked(value):
    return jnp.concatenate(split(value), axis=0)


def folded(value):
    rows = value.shape[0] // 2
    return value[:rows] + value[rows:]


def kernel(chips, sides, cores, source_ref, inside_ref, upper_hbm, lower_hbm, upper_gain, lower_gain,
           field_ref, reflected_ref,
           stage, upper, lower, gathered, down_ref, sums, core_out, core_in, work, ring_in,
           load_sem, core_send, core_recv, ring_send, ring_recv, pair_send, pair_recv, pass_send, pass_recv):
    columns, size = source_ref.shape
    lines, half = chips // sides, columns // 2
    middle = chips // 2
    me = lax.axis_index("row")
    core = lax.rem(me, cores)
    side = lax.rem(me // cores, sides)
    line = me // (cores * sides)
    place = side * (chips - 1 - line) + (1 - side) * line

    def at(hops, dc):
        there = lax.rem(place + hops + chips, chips)
        turned = there // lines
        row = turned * (chips - 1 - there) + (1 - turned) * there
        return (row * sides + turned) * cores + lax.rem(core + dc, cores)

    def slot_of(k, dc):
        return k * cores + dc

    def rows(chunk):
        return pl.ds(chunk * half, half)

    def reach(way, chunk):
        return middle if way == chunk else chips - 1 - middle

    pairs = [(way, chunk) for chunk in range(2) for way in range(2)]
    step_of = (1, -1)
    visit = [0]
    for near in range(1, middle):
        visit += [near, chips - near]
    visit += [middle]

    def load(operator, which, k, dc):
        slot = slot_of(k, dc)
        wanted = pl.ds(pl.multiple_of(at(-k, dc) * size, size), size)
        copy = pltpu.make_async_copy(operator.at[:, wanted], stage.at[slot], load_sem.at[which, slot])
        copy.start()
        return copy

    upper_loads = {slot_of(k, dc): load(upper_hbm, 0, k, dc) for k in visit for dc in range(cores)}

    partners = [at(0, 1), at(1, 0), at(-1, 0)]
    barrier = pltpu.get_barrier_semaphore()
    for partner in partners:
        pl.semaphore_signal(barrier, inc=1, device_id={"row": partner}, device_id_type=MESH)
    pl.semaphore_wait(barrier, len(partners))

    started = []

    def send(src, dst, send_sem, recv_sem, target):
        copy = pltpu.make_async_remote_copy(
            src_ref=src, dst_ref=dst, send_sem=send_sem, recv_sem=recv_sem,
            device_id={"row": target}, device_id_type=MESH)
        copy.start()
        started.append(copy)
        return copy

    def gather_apply(phase, own, parts, loads, after):
        ring, pair = {}, {}
        chunk_rows = min(256, size)

        def hop(way, chunk, distance):
            k = distance if way == 0 else chips - distance
            before = k - 1 if way == 0 else (k + 1) % chips
            src = own if distance == 1 else gathered.at[phase, slot_of(before, 0)]
            ring[way, chunk, distance] = send(
                src.at[rows(chunk)], gathered.at[phase, slot_of(k, 0), rows(chunk)],
                ring_send.at[phase, k, chunk], ring_recv.at[phase, k, chunk], at(step_of[way], 0))

        def share(k):
            src = gathered.at[phase, slot_of(k, 0)] if k else own
            pair[k] = send(src, gathered.at[phase, slot_of(k, 1)], pair_send.at[phase, k],
                           pair_recv.at[phase, k], at(0, 1))

        groups = [[(0, 0)], [(0, 1)]]
        for distance in range(1, middle + 1):
            here = sorted({distance, chips - distance})
            groups += [[(k, dc) for k in here] for dc in range(cores)]

        def divide(k, dc):
            slot = slot_of(k, dc)
            for begin in range(0, size, chunk_rows):
                high, low = split(stage[slot, begin:begin + chunk_rows, :])
                parts[slot, begin:begin + chunk_rows, :] = high
                parts[slot, size + begin:size + begin + chunk_rows, :] = low

        def add(keys):
            following = groups[groups.index(keys) + 1] if keys != groups[-1] else []
            for k, dc in keys:
                if dc:
                    pair[k].wait_recv()
            for key in following:
                loads[slot_of(*key)].wait()
            total = None
            for place_of, (k, dc) in enumerate(keys):
                slot = slot_of(k, dc)
                if place_of < len(following):
                    divide(*following[place_of])
                both = stacked(gathered[phase, slot] if slot else own[...])
                term = folded(lax.dot_general(parts[slot], both, NT, preferred_element_type=F32))
                total = term if total is None else total + term
            for key in following[len(keys):]:
                divide(*key)
            if keys == groups[0]:
                sums[...] = total
            else:
                sums[...] += total
            for key in following:
                after(*key)

        for way, chunk in pairs:
            hop(way, chunk, 1)
        share(0)
        loads[0].wait()
        divide(0, 0)
        after(0, 0)
        add([(0, 0)])
        late = [(0, 1)]
        for distance in range(1, middle + 1):
            here = sorted({distance, chips - distance})
            for way, chunk in pairs:
                if chunk == 1 and way == 0 and late:
                    add(late)
                    late = []
                if distance <= reach(way, chunk):
                    ring[way, chunk, distance].wait_recv()
                    if distance < reach(way, chunk):
                        hop(way, chunk, distance + 1)
            for k in here:
                share(k)
            add([(k, 0) for k in here])
            late = [(k, 1) for k in here]
        add(late)
        return folded(sums[...].T)

    def scatter_apply(phase, value, parts):
        both = stacked(value)
        both = jnp.concatenate([both, both], axis=1)

        def part(k, dc):
            return folded(lax.dot_general(both, parts[slot_of(k, dc)], NN, preferred_element_type=F32))

        pair, ring = {}, {}

        def compute(keys):
            others = [part(k, 1) for k in keys]
            for k, other in zip(keys, others):
                core_out[phase, k] = other
                pair[k] = send(core_out.at[phase, k], core_in.at[phase, k], core_send.at[phase, k],
                               core_recv.at[phase, k], at(0, 1))
            for k in keys:
                work[phase, k] = part(k, 0)

        def pass_on(distance):
            for k in sorted({distance, chips - distance}):
                pair[k].wait_recv()
                work[phase, k] = work[phase, k] + core_in[phase, k]
            for way, chunk in pairs:
                if distance > reach(way, chunk):
                    continue
                k = chips - distance if way == 0 else distance
                if distance < reach(way, chunk):
                    ring[way, chunk, distance].wait_recv()
                    work[phase, k, rows(chunk)] = work[phase, k, rows(chunk)] + ring_in[phase, way, distance, rows(chunk)]
                ring[way, chunk, distance - 1] = send(
                    work.at[phase, k, rows(chunk)], ring_in.at[phase, way, distance - 1, rows(chunk)],
                    pass_send.at[phase, way, distance - 1, chunk], pass_recv.at[phase, way, distance - 1, chunk],
                    at(step_of[way], 0))

        compute([middle])
        for distance in range(middle - 1, -1, -1):
            compute(sorted({distance, (chips - distance) % chips}))
            pass_on(distance + 1)
        pair[0].wait_recv()
        total = work[phase, 0] + core_in[phase, 0]
        for way, chunk in pairs:
            ring[way, chunk, 0].wait_recv()
        return total + ring_in[phase, 0, 0] + ring_in[phase, 1, 0]

    lower_loads = {}

    def load_lower(k, dc):
        lower_loads[slot_of(k, dc)] = load(lower_hbm, 1, k, dc)

    down_ref[...] = gather_apply(0, source_ref, upper, upper_loads, load_lower)
    field = gather_apply(1, down_ref, lower, lower_loads, lambda k, dc: None)
    field_ref[...] = field
    scaled = lower_gain[...] * field + inside_ref[...]
    bounced = scatter_apply(0, scaled, lower)
    mixed = upper_gain[...] * bounced - down_ref[...]
    reflected_ref[...] = scatter_apply(1, mixed, upper)
    for copy in started:
        copy.wait_send()


def body(devices, sources, lower_sources, upper_operator, lower_operator, upper_impedance, lower_impedance):
    batch_count, column_count, size = sources.shape
    columns = batch_count * column_count
    cores, sides = 2, 2
    chips = devices // cores
    middle = chips // 2
    vmem, dma = pltpu.VMEM, pltpu.SemaphoreType.DMA
    traces = jax.ShapeDtypeStruct((columns, size), F32)
    whole = pl.BlockSpec(memory_space=pltpu.VMEM)
    remote = pl.BlockSpec(memory_space=pl.ANY)
    field, reflected = pl.pallas_call(
        functools.partial(kernel, chips, sides, cores),
        out_shape=(traces, traces),
        in_specs=[whole, whole, remote, remote, whole, whole],
        out_specs=(whole, whole),
        scratch_shapes=[
            vmem((devices, size, size), F32),
            vmem((devices, 2 * size, size), BF16),
            vmem((devices, 2 * size, size), BF16),
            vmem((2, devices, columns, size), F32),
            vmem((columns, size), F32),
            vmem((size, 2 * columns), F32),
            vmem((2, chips, columns, size), F32),
            vmem((2, chips, columns, size), F32),
            vmem((2, chips, columns, size), F32),
            vmem((2, 2, middle, columns, size), F32),
            dma((2, devices)),
            dma((2, chips)),
            dma((2, chips)),
            dma((2, chips, 2)),
            dma((2, chips, 2)),
            dma((2, chips)),
            dma((2, chips)),
            dma((2, 2, middle, 2)),
            dma((2, 2, middle, 2)),
        ],
        compiler_params=pltpu.CompilerParams(
            collective_id=0, has_side_effects=True, vmem_limit_bytes=60 * 1024 * 1024),
    )(
        sources.reshape(columns, size),
        lower_sources.reshape(columns, size),
        upper_operator,
        lower_operator,
        upper_impedance.reshape(1, size),
        lower_impedance.reshape(1, size),
    )
    shape = (batch_count, column_count, size)
    return field.reshape(shape), reflected.reshape(shape)


def solution(mesh):
    placed = (
        P("group", None, "row"),
        P("group", None, "row"),
        P(("group", "row"), None),
        P(("group", "row"), None),
        P(("group", "row")),
        P(("group", "row")),
    )
    return jax.shard_map(
        functools.partial(body, mesh.shape["row"]),
        mesh=mesh,
        in_specs=placed,
        out_specs=(P("group", None, "row"), P("group", None, "row")),
        check_vma=False,
    )
```

time: 274 us -> 69.1 us (0.25)
  waiting for transfers between devices: 193 us -> 0 us
  matrix products: 65.9 us -> 0 us
  Pallas kernels: 0 us -> 65.3 us
  between operations: 13.8 us -> 0.64 us
  local copies, waits for them, and re-layouts: 0.02 us -> 2.95 us
    reduce_scatter x2 -> x0, waiting for transfers between devices: 113 us -> none  [the longest x1 56.5 us: body(): lax.psum_scatter(transposed_term(upper_operator, mixed), 'row', scatter_d...]
    all_gather x2 -> x0, waiting for transfers between devices: 79.7 us -> none  [the longest x1 42.9 us: body(): lax.all_gather(entering, 'row', axis=1, tiled=True)]
    dot_general x4 -> x0, matrix products: 65.9 us -> none  [the longest x2 37.9 us: apply_rows(): lax.dot_general(piece, operator, (((1,), (1,)), ((), ())), precision=lax....]
    pallas_call x0 -> x1, Pallas kernels: none -> 65.3 us  [body(): pl.pallas_call(functools.partial(kernel, chips, sides, cores), out_shape=...]
    unnamed x8 -> x2, local copies, waits for them, and re-layouts: 0.02 us -> 2.95 us
  transfers between devices with their start and end apart: 4 -> 0, of which waited for: 4 -> 0; matrix products, arithmetic and copies ran while one was open for 0% -> 0% of each run, Pallas kernels for 0% -> 0%
where the time goes in v3:
time: 69.1 us; the launch traced here: 68.9 us
  Pallas kernels  65.3 us (95%)
  local copies, waits for them, and re-layouts  2.95 us (4%)
    pallas_call x1, Pallas kernels, body(): pl.pallas_call(functools.partial(kernel, chips, sides, cores), out_shape=...  65.3 us
    unnamed x2, local copies, waits for them, and re-layouts  2.95 us

profile of v3, /device:TPU:0, one launch (start us, length us, event | category | flops | bytes accessed | tf_op | source)
XLA Modules:
  0.0 68.9 jit_solution(4234311099360041229)
XLA Ops:
  0.6 65.3 %shard_map.77 = (f32[32,512]{1,0:T(8,128)}, f32[32,512]{1,0:T(8,128)}) custom-call(f32[32,512]{1,0:T(8,128)} %bitcast.6, f32[32,512]{1,0:T(8,128)} %bitcast.7, f32[512,8192]{1,0:T(8,128)} %upper_hbm.1, f32[512,8192]{1,0:T(8,128)} %lower_hbm.1, f32[1,512]{1,0:T(1,128)} %bitcast.10, f32[1,512]{1,0:T(1,128)} %bitcast.11), custom_call_target="tpu_custom_call" | custom-call | tf_op jit(solution)/shard_map/pallas_call | solution.py:238
  65.9 1.5 %copy.10 = f32[2,16,512]{2,1,0:T(8,128)} copy(f32[2,16,512]{2,1,0:T(8,128)} %bitcast.9) | data formatting | bytes 131072
  67.4 1.5 %copy.11 = f32[2,16,512]{2,1,0:T(8,128)} copy(f32[2,16,512]{2,1,0:T(8,128)} %bitcast.8) | data formatting | bytes 131072
